TPU v7x, 128 devices: a whole 4x4x4 slice. The times are simulated.
128 devices in a mesh: row: 8 (over y_hi, x), col: 16 (over y_lo, z, core).
Axes of the slice: x: 4, y: 4 (y_hi: 2, y_lo: 2; y = y_hi * 2 + y_lo), z: 4, core: 2. Of those that a mesh axis runs over, the one named last changes fastest.
Arguments:
- top_coeffs: float32 [8, 131072], P(None, ('row', 'col')), may hold values from -6 to 6
- fresh_one: bfloat16 [56, 131072], P(None, ('row', 'col')), may hold values from -6 to 6
- fresh_two: bfloat16 [56, 8, 131072], P(None, None, ('row', 'col')), may hold values from -6 to 6
- fresh_three: bfloat16 [56, 64, 131072], P(None, None, ('row', 'col')), may hold values from -6 to 6
- mixing: bfloat16 [64, 64], replicated, may hold values from -0.75 to 0.75
- transfer: float32 [2048, 2048], P(None, 'col'), may hold values from 0.1 to 1, as said below
Outputs:
- density: float32 [16, 2048, 2048], P('row', 'col')
Inputs may be any that keep to these rules, and one draw needn't show every extreme that they name: transfer is even: its value at the positions of modes (ky, kz) equals its value at the positions of modes (-ky mod 2048, -kz mod 2048).
All inputs are finite; a program needn't handle non-finite values.
Results may differ from a plain program's by a relative error of at most 0.0003.
Values sent between devices are 32-bit elements; how exact they have to be, the bound alone decides.
A program may use at most 192 MiB of HBM per device.

v0:
```python
import functools
import math

import jax
import jax.numpy as jnp
import numpy as np
from jax import lax
from jax.experimental import pallas as pl
from jax.experimental.pallas import tpu as pltpu
from jax.sharding import PartitionSpec as P

F32 = jnp.float32
BF16 = jnp.bfloat16
VMEM = pltpu.VMEM


def two_terms(values):
    values = np.asarray(values, np.float32)
    high = values.astype(jnp.bfloat16)
    low = (values - high.astype(np.float32)).astype(jnp.bfloat16)
    return high, low


def bit(value, index):
    return (value >> index) & 1


def owner_tables():
    row = np.arange(64)
    pick_one = np.zeros((64, 64), np.float32)
    pick_one[row, 8 * (row % 8) + row // 8] = 1
    row = np.arange(512)
    cell, coef, parent = row % 8, (row >> 4) & 7, 2 * (row >> 7) + bit(row, 3)
    pick_two = np.zeros((512, 64), np.float32)
    pick_two[row, 8 * cell + coef] = 1
    column = np.arange(512)
    source = np.where(column < 448, 8 + column // 8, (column - 448) // 8)
    spread_two = np.zeros((64, 512), np.float32)
    spread_two[source, column] = 1
    mask_two = (column[None, :] % 8 == parent[:, None]).astype(np.float32)
    row = np.arange(128)
    c2x, c3x, c2y, c3y, c1z, c2z, c3z = [bit(row, 6 - i) for i in range(7)]
    pick_three = np.zeros((128, 64), np.float32)
    pick_three[row, 8 * (4 * c3x + 2 * c3y + c3z)] = 1
    column = np.arange(1024)
    source = np.where(column < 896, 8 + column // 16, (column - 896) // 16)
    spread_three = np.zeros((64, 1024), np.float32)
    spread_three[source, column] = 1
    own = 8 * c1z + 4 * c2x + 2 * c2y + c2z
    mask_three = (column[None, :] % 16 == own[:, None]).astype(np.float32)
    picks = [pick_one, pick_two, spread_two, mask_two, pick_three, spread_three, mask_three]
    return [np.asarray(each, jnp.bfloat16) for each in picks]


def slot_tables():
    slot = np.arange(128)
    y_part = 2 * (slot // 32) + slot % 2
    z_part = (slot // 2) % 16
    mode = np.arange(128)
    kz, ky = mode // 8, mode % 8
    angle = 2 * np.pi * (np.outer(kz, z_part) / 16 + np.outer(ky, y_part) / 8)
    high, low = two_terms(np.concatenate([np.cos(angle), np.sin(angle)], axis=1))
    both = np.concatenate([high, low], axis=0)
    turn = 2 * np.pi * np.outer(np.arange(4), y_part) / 32
    turns = np.stack([np.cos(turn), np.sin(turn)]).astype(np.float32)
    return both, turns


def line_tables():
    z_low = np.arange(128)
    out = []
    for kz_low in range(16):
        angle = 2 * np.pi * np.outer(z_low, kz_low + 16 * np.arange(128)) / 2048
        cos, sin = np.cos(angle), np.sin(angle)
        out.append(np.block([[cos, -sin], [sin, cos]]))
    return np.stack(two_terms(np.stack(out)), axis=1)


def turn_tables():
    kt = np.arange(4)[:, None]
    s = np.arange(8)[None, :]
    ky_low = kt + 4 * s
    one = 2 * np.pi * ky_low[:, None, :] * np.arange(8)[None, :, None] / 256
    mode = ky_low[:, None, None, :] + 32 * np.arange(8)[None, None, :, None]
    two = 2 * np.pi * mode * np.arange(8)[None, :, None, None] / 2048
    wide = lambda a: np.ascontiguousarray(
        np.broadcast_to(np.stack([np.cos(a), np.sin(a)])[..., None], (2,) + a.shape + (128,))
    ).astype(np.float32)
    return wide(one), wide(two)


def digit_tables():
    out = []
    for pair in range(2):
        full = np.zeros((2, 2, 8, 8, 2, 2, 8, 8))
        for k in range(2):
            y2a = np.arange(8)[:, None]
            s = np.arange(8)[None, :]
            angle = 2 * np.pi * (s * y2a / 8 + (2 * pair + k) * y2a / 32)
            cos, sin = np.cos(angle), np.sin(angle)
            for y0 in range(8):
                full[0, k, :, y0, 0, k, y0, :] = cos
                full[0, k, :, y0, 1, k, y0, :] = -sin
                full[1, k, :, y0, 0, k, y0, :] = sin
                full[1, k, :, y0, 1, k, y0, :] = cos
        high, low = two_terms(full.reshape(256, 256))
        out.append(np.concatenate([high, low], axis=0))
    return np.stack(out)


def split(x):
    high = x.astype(BF16)
    return high, (x - high.astype(F32)).astype(BF16)


def dot(a, b):
    return jnp.dot(a, b, preferred_element_type=F32)


def dot_nt(a, b):
    return lax.dot_general(a, b, (((1,), (1,)), ((), ())), preferred_element_type=F32)


def add(a, b):
    return (a[0] + b[0], a[1] + b[1])


def sub(a, b):
    return (a[0] - b[0], a[1] - b[1])


def times(a, cos, sin, sign):
    if sign > 0:
        return (a[0] * cos - a[1] * sin, a[1] * cos + a[0] * sin)
    return (a[0] * cos + a[1] * sin, a[1] * cos - a[0] * sin)


def quarter(a, sign):
    return (-a[1], a[0]) if sign > 0 else (a[1], -a[0])


def add_quarter(a, b, sign):
    return (a[0] - b[1], a[1] + b[0]) if sign > 0 else (a[0] + b[1], a[1] - b[0])


def four(x, sign):
    even, odd = add(x[0], x[2]), add(x[1], x[3])
    left, right = sub(x[0], x[2]), sub(x[1], x[3])
    return [add(even, odd), add_quarter(left, right, sign), sub(even, odd),
            add_quarter(left, right, -sign)]


def eight(x, sign):
    even = four([x[0], x[2], x[4], x[6]], sign)
    odd = four([x[1], x[3], x[5], x[7]], sign)
    half = math.sqrt(0.5)
    a = odd[1]
    if sign > 0:
        odd1 = ((a[0] - a[1]) * half, (a[1] + a[0]) * half)
    else:
        odd1 = ((a[0] + a[1]) * half, (a[1] - a[0]) * half)
    a = odd[3]
    if sign > 0:
        odd3 = ((-a[0] - a[1]) * half, (a[0] - a[1]) * half)
    else:
        odd3 = ((a[1] - a[0]) * half, (-a[0] - a[1]) * half)
    return [
        add(even[0], odd[0]),
        add(even[1], odd1),
        add_quarter(even[2], odd[2], sign),
        add(even[3], odd3),
        sub(even[0], odd[0]),
        sub(even[1], odd1),
        add_quarter(even[2], odd[2], -sign),
        sub(even[3], odd3),
    ]


def sixteen(x, sign):
    out = [None] * 16
    mid = [four([x[a], x[a + 4], x[a + 8], x[a + 12]], sign) for a in range(4)]
    for c in range(4):
        terms = []
        for a in range(4):
            angle = 2 * math.pi * a * c / 16
            if a * c == 0:
                terms.append(mid[a][c])
            elif a * c == 4:
                terms.append(quarter(mid[a][c], sign))
            else:
                terms.append(times(mid[a][c], math.cos(angle), math.sin(angle), sign))
        done = four(terms, sign)
        for d in range(4):
            out[c + 4 * d] = done[d]
    return out


def owner_kernel(top, one, two, three, mixing, pick_one, pick_two, spread_two, mask_two,
                 pick_three, spread_three, mask_three, slots, turns, out,
                 parents, leaf_map, leaves, high_rows, low_rows):
    step = pl.program_id(0)

    @pl.when(step == 0)
    def _():
        mix = mixing[...]
        first = dot(pick_one[...], mix).astype(BF16)
        high, low = split(jnp.concatenate([top[...], one[...].astype(F32)], axis=0))
        level_one = dot(first, high) + dot(first, low)
        rows = dot(pick_two[...], mix).astype(BF16)
        second = (dot(rows, spread_two[...]) * mask_two[...].astype(F32)).astype(BF16)
        high, low = split(level_one)
        level_two = dot(second, jnp.concatenate([two[...], high], axis=0))
        level_two = level_two + dot(second[:, 384:], jnp.concatenate([jnp.zeros_like(low), low], axis=0))
        for tile in range(4):
            high, low = split(level_two[tile * 128:(tile + 1) * 128])
            parents[tile, 0:128] = high
            parents[tile, 128:256] = low
        rows = dot(pick_three[...], mix).astype(BF16)
        leaf_map[...] = (dot(rows, spread_three[...]) * mask_three[...].astype(F32)).astype(BF16)

    draws = three[...].reshape(896, 1024)
    got = dot(leaf_map[:, :896], draws)
    near = parents[step]
    got = got + dot(leaf_map[:, 896:], near[:128]) + dot(leaf_map[:, 896:], near[128:])
    half = lax.rem(step, 2)
    for group in range(4):
        leaves[group, half] = got[group * 32:(group + 1) * 32]

    @pl.when(half == 1)
    def _():
        for e in range(2):
            for pair in range(2):
                quarters = []
                for t in range(4):
                    lane = (4 * e + t) * 128
                    re = leaves[2 * pair, :, :, lane:lane + 128].reshape(64, 128)
                    im = leaves[2 * pair + 1, :, :, lane:lane + 128].reshape(64, 128)
                    quarters.append((re, im))
                for k, value in enumerate(four(quarters, -1)):
                    if k:
                        value = times(value, turns[0, k:k + 1], turns[1, k:k + 1], -1)
                    re_high, re_low = split(value[0])
                    im_high, im_low = split(value[1])
                    base = pair * 128
                    high_rows[k, base:base + 64, 0:128] = re_high
                    high_rows[k, base:base + 64, 128:256] = im_high
                    high_rows[k, base + 64:base + 128, 0:128] = im_high
                    high_rows[k, base + 64:base + 128, 128:256] = -re_high
                    low_rows[k, base:base + 64, 0:128] = re_low
                    low_rows[k, base:base + 64, 128:256] = im_low
                    low_rows[k, base + 64:base + 128, 0:128] = im_low
                    low_rows[k, base + 64:base + 128, 128:256] = -re_low
            for k in range(4):
                both = dot_nt(slots[...], high_rows[k])
                done = both[:128] + both[128:] + dot_nt(slots[0:128], low_rows[k])
                for pair in range(2):
                    place = 4 * e + 2 * (step // 2) + pair
                    piece = done[:, pair * 128:(pair + 1) * 128].reshape(16, 8, 128)
                    out[place, :, k] = piece


def owners(top, one, two, three, mixing):
    tables = owner_tables()
    slots, turns = slot_tables()
    whole = lambda a: pl.BlockSpec(a.shape, lambda i: (0,) * a.ndim)
    two = two.reshape(448, 1024)
    operands = [top, one, two, three, mixing] + [jnp.asarray(t) for t in tables]
    operands += [jnp.asarray(slots), jnp.asarray(turns)]
    specs = [whole(a) for a in operands]
    specs[3] = pl.BlockSpec((56, 16, 1024), lambda i: (0, i, 0))
    return pl.pallas_call(
        owner_kernel,
        grid=(4,),
        in_specs=specs,
        out_specs=pl.BlockSpec((8, 16, 4, 8, 128), lambda i: (0, 0, 0, 0, 0)),
        out_shape=jax.ShapeDtypeStruct((8, 16, 4, 8, 128), F32),
        scratch_shapes=[
            VMEM((4, 256, 1024), BF16),
            VMEM((128, 1024), BF16),
            VMEM((4, 2, 32, 1024), F32),
            VMEM((4, 256, 256), BF16),
            VMEM((4, 256, 256), BF16),
        ],
        compiler_params=pltpu.CompilerParams(vmem_limit_bytes=56 * 2**20),
    )(*operands)


def owner_index(q, w):
    index = 0
    for b in range(4):
        index += bit(w, b) << (2 * b)
    for b in range(3):
        index += bit(q, b) << (2 * b + 1)
    return index


def swap_lanes(x, lane):
    for b in range(4):
        width = 8 << b
        keep = (lane & width) == 0
        y = list(x)
        for i in range(16):
            if not bit(i, b):
                j = i | (1 << b)
                y[i] = jnp.where(keep, x[i], pltpu.roll(x[j], width, 1))
                y[j] = jnp.where(keep, pltpu.roll(x[i], 128 - width, 1), x[j])
        x = y
    return x


def line_kernel(arrived, transfer, lines, turn_one, turn_two, digits, out,
                factor, table, sem, flat, mid, work, spread, lined):
    col = lax.axis_index("col")
    fetch = pltpu.make_async_copy(lines.at[col], table, sem)
    fetch.start()

    @pl.loop(0, 128)
    def _(i):
        low, kt, high = i // 32, (i // 8) % 4, i % 8
        rows = transfer[pl.ds(pl.multiple_of((low * 4 + kt) * 128 + high * 16, 16), 16), :]
        factor[pl.ds((kt * 8 + high) * 64 + low, 16, stride=4), :] = rows * (1.0 / (2048 * 2048))

    fetch.wait()
    lane = lax.broadcasted_iota(jnp.int32, (8, 128), 1)

    @pl.loop(0, 4)
    def _(kt):
        for q in range(8):
            got = swap_lanes([arrived[owner_index(q, w), kt] for w in range(16)], lane)
            for oy in range(8):
                flat[pl.ds((q * 8 + oy) * 8, 8), 0:128] = got[oy]
                flat[pl.ds((q * 8 + oy) * 8, 8), 128:256] = got[8 + oy]
        for part in range(2):
            rows = pl.ds(part * 256, 256)
            high, low = split(flat[rows, :])
            mid[rows, :] = dot(high, table[0]) + dot(low, table[0]) + dot(high, table[1])

        @pl.loop(0, 8)
        def _(oy):
            x = []
            for q in range(8):
                rows = pl.ds(pl.multiple_of(q * 64 + oy * 8, 8), 8)
                value = (mid[rows, 0:128], mid[rows, 128:256])
                if q:
                    value = times(value, turn_one[0, kt, q], turn_one[1, kt, q], -1)
                x.append(value)
            for k, value in enumerate(eight(x, -1)):
                value = times(value, turn_two[0, kt, oy, k], turn_two[1, kt, oy, k], -1)
                work[0, k, oy] = value[0]
                work[1, k, oy] = value[1]

        @pl.loop(0, 8)
        def _(kq):
            x = eight([(work[0, kq, oy], work[1, kq, oy]) for oy in range(8)], -1)
            y = []
            for k in range(8):
                rows = pl.ds(pl.multiple_of((kt * 8 + k) * 64 + kq * 8, 8), 8)
                scale = factor[rows, :]
                y.append((x[k][0] * scale, x[k][1] * scale))
            for y0, value in enumerate(eight(y, 1)):
                value = times(value, turn_two[0, kt, y0, kq], turn_two[1, kt, y0, kq], 1)
                work[0, kq, y0] = value[0]
                work[1, kq, y0] = value[1]

        @pl.loop(0, 8)
        def _(y0):
            x = [(work[0, kq, y0], work[1, kq, y0]) for kq in range(8)]
            for y1, value in enumerate(eight(x, 1)):
                if y1:
                    value = times(value, turn_one[0, kt, y1], turn_one[1, kt, y1], 1)
                spread[0, kt, y1, y0] = value[0]
                spread[1, kt, y1, y0] = value[1]

    @pl.loop(0, 4)
    def _(pair):
        got = []
        for ktp in range(2):
            columns = []
            for one in range(2):
                pieces = [
                    spread[part, 2 * ktp + k, 2 * pair + one].reshape(64, 128)
                    for part in range(2)
                    for k in range(2)
                ]
                columns.append(jnp.concatenate(pieces, axis=0))
            high, low = split(jnp.concatenate(columns, axis=1))
            both = dot(digits[ktp], high)
            got.append(both[:256] + both[256:] + dot(digits[ktp, 0:256], low))
        for y2a in range(8):
            for one in range(2):
                x = []
                for kt in range(4):
                    base = (kt % 2) * 64 + y2a * 8
                    tile = got[kt // 2]
                    lanes = slice(one * 128, one * 128 + 128)
                    x.append((tile[base:base + 8, lanes], tile[128 + base:128 + base + 8, lanes]))
                for y2b, value in enumerate(four(x, 1)):
                    rows = pl.ds(pl.multiple_of((y2b * 8 + y2a) * 64 + (2 * pair + one) * 8, 8), 8)
                    lined[rows, 0:128] = value[0]
                    lined[rows, 128:256] = value[1]

    @pl.loop(0, 8)
    def _(chunk):
        high, low = split(lined[pl.ds(pl.multiple_of(chunk * 256, 256), 256), :])
        done = dot_nt(high, table[0]) + dot_nt(low, table[0]) + dot_nt(high, table[1])
        for half in range(2):
            for part in range(2):
                out[2 * chunk + half, part] = done[half * 128:half * 128 + 128,
                                                   part * 128:part * 128 + 128]


def along_lines(arrived, transfer):
    lines = jnp.asarray(line_tables())
    turn_one, turn_two = (jnp.asarray(t) for t in turn_tables())
    digits = jnp.asarray(digit_tables())
    inside = pl.BlockSpec(memory_space=VMEM)
    return pl.pallas_call(
        line_kernel,
        in_specs=[inside, inside, pl.BlockSpec(memory_space=pl.ANY), inside, inside, inside],
        out_specs=inside,
        out_shape=jax.ShapeDtypeStruct((16, 2, 128, 128), F32),
        scratch_shapes=[
            VMEM((2048, 128), F32),
            VMEM((2, 256, 256), BF16),
            pltpu.SemaphoreType.DMA,
            VMEM((512, 256), F32),
            VMEM((512, 256), F32),
            VMEM((2, 8, 8, 8, 128), F32),
            VMEM((2, 4, 8, 8, 8, 128), F32),
            VMEM((2048, 256), F32),
        ],
        compiler_params=pltpu.CompilerParams(vmem_limit_bytes=56 * 2**20),
    )(arrived, transfer, lines, turn_one, turn_two, digits)


def strip_kernel(arrived, out):
    @pl.loop(0, 16)
    def _(tile):
        rows = pl.ds(pl.multiple_of(tile * 8, 8), 8)
        x = [(arrived[k, 0, rows, :], arrived[k, 1, rows, :]) for k in range(16)]
        for z, value in enumerate(sixteen(x, 1)):
            out[0, rows, z * 128:(z + 1) * 128] = value[0]
            out[1, rows, z * 128:(z + 1) * 128] = value[1]


def strips(arrived):
    inside = pl.BlockSpec(memory_space=VMEM)
    return pl.pallas_call(
        strip_kernel,
        in_specs=[inside],
        out_specs=inside,
        out_shape=jax.ShapeDtypeStruct((2, 128, 2048), F32),
        compiler_params=pltpu.CompilerParams(vmem_limit_bytes=32 * 2**20),
    )(arrived)


def body(top, one, two, three, mixing, transfer):
    sent = owners(top, one, two, three, mixing).reshape(128, 32, 128)
    arrived = lax.all_to_all(sent, ("row", "col"), split_axis=0, concat_axis=0, tiled=True)
    lines = along_lines(arrived.reshape(128, 4, 8, 128), transfer)
    back = lax.all_to_all(lines, "col", split_axis=0, concat_axis=0, tiled=True)
    return strips(back)


def solution(mesh):
    return jax.shard_map(
        body,
        mesh=mesh,
        in_specs=(
            P(None, ("row", "col")),
            P(None, ("row", "col")),
            P(None, None, ("row", "col")),
            P(None, None, ("row", "col")),
            P(),
            P(None, "col"),
        ),
        out_specs=P("row", "col", None),
        check_vma=False,
    )
```

profile of v0, /device:TPU:1, one launch (start us, length us, event | category | flops | bytes accessed | tf_op | source)
XLA Modules:
  0.0 102.4 jit_solution(12853050542892954989)
XLA Ops:
  0.0 10.8 %shard_map.181 = f32[8,16,4,8,128]{4,3,2,1,0:T(8,128)} custom-call(f32[8,1024]{1,0:T(8,128)} %top.1, bf16[56,1024]{1,0:T(8,128)(2,1)} %one.1, bf16[448,1024]{1,0:T(8,128)(2,1)} %bitcast.5, bf16[56,64,1024]{2,1,0:T(8,128)(2,1)} %three.1, bf16[64,64]{1,0:T(8,128)(2,1)} %mixing.1, bf16[64,64]{1,0:T(8,128)(2,1)} %constant.26.clone.pick_one, ...), custom_call_target="tpu_custom_call" | custom-call | tf_op jit(solution)/shard_map/pallas_call | solution.py:271
  10.8 42.3 %all_to_all.10 = f32[128,32,128]{2,1,0:T(8,128)} all-to-all(f32[128,32,128]{2,1,0:T(8,128)} %bitcast.3), channel_id=1, replica_groups=mesh['row'=8,'col'=16] {'row','col'}, dimensions={0} | all-to-all | bytes 4194304 | tf_op jit(solution)/shard_map/all_to_all | solution.py:459
  53.1 16.6 %shard_map.182 = f32[16,2,128,128]{3,2,1,0:T(8,128)} custom-call(f32[128,4,8,128]{3,2,1,0:T(8,128)} %bitcast.4, f32[2048,128]{1,0:T(8,128)} %transfer.1, bf16[16,2,256,256]{3,2,1,0:T(8,128)(2,1)} %constant.35.clone.lines, f32[2,4,8,8,128]{4,3,2,1,0:T(8,128)} %constant.36.clone.turn_one, f32[2,4,8,8,8,128]{5,4,3,2,1,0:T(8,128)} %constant.37.clone.turn_two, ...), custom_call_target="tpu_custom_call" | custom-call | tf_op jit(solution)/shard_map/pallas_call | solution.py:417
  69.7 30.8 %all_to_all.11.arrived = f32[16,2,128,128]{3,2,1,0:T(8,128)S(1)} all-to-all(f32[16,2,128,128]{3,2,1,0:T(8,128)} %shard_map.182), channel_id=1, replica_groups=mesh['row'=8,'col'=16] {'col'}, dimensions={0} | all-to-all | bytes 4194304 | tf_op jit(solution)/shard_map/all_to_all | solution.py:461
  100.4 1.9 %shard_map.183 = f32[2,128,2048]{2,1,0:T(8,128)} custom-call(f32[16,2,128,128]{3,2,1,0:T(8,128)S(1)} %all_to_all.11.arrived), custom_call_target="tpu_custom_call" | custom-call | tf_op jit(solution)/shard_map/pallas_call | solution.py:448
where the time goes:
time: 103 us; the launch traced here: 102 us
  blocking collectives  73.1 us (71%)
  Pallas kernels  29.3 us (28%)
    all_to_all x1, blocking collectives, body(): lax.all_to_all(sent, ('row', 'col'), split_axis=0, concat_axis=0, tiled=T...  42.3 us
    all_to_all x1, blocking collectives, body(): back = lax.all_to_all(lines, 'col', split_axis=0, concat_axis=0, tiled=True)  30.8 us
    pallas_call x1, Pallas kernels, along_lines(): pl.pallas_call(line_kernel, in_specs=[inside, inside, pl.BlockSpec(memory...  16.6 us
    pallas_call x1, Pallas kernels, owners(): pl.pallas_call(owner_kernel, grid=(4,), in_specs=specs, out_specs=pl.Bloc...  10.8 us

commit v1 on v0

v1 whole, which is shorter than its diff:
```python
import math

import jax
import jax.numpy as jnp
import numpy as np
from jax import lax
from jax.experimental import pallas as pl
from jax.experimental.pallas import tpu as pltpu
from jax.sharding import PartitionSpec as P

F32 = jnp.float32
BF16 = jnp.bfloat16
VMEM = pltpu.VMEM
MESH = pl.DeviceIdType.MESH


def two_terms(values):
    values = np.asarray(values, np.float32)
    high = values.astype(jnp.bfloat16)
    low = (values - high.astype(np.float32)).astype(jnp.bfloat16)
    return high, low


def bit(value, index):
    return (value >> index) & 1


def owner_tables():
    row = np.arange(64)
    pick_one = np.zeros((64, 64), np.float32)
    pick_one[row, 8 * (row % 8) + row // 8] = 1
    row = np.arange(512)
    cell, coef, parent = row % 8, (row >> 4) & 7, 2 * (row >> 7) + bit(row, 3)
    pick_two = np.zeros((512, 64), np.float32)
    pick_two[row, 8 * cell + coef] = 1
    column = np.arange(512)
    source = np.where(column < 448, 8 + column // 8, (column - 448) // 8)
    spread_two = np.zeros((64, 512), np.float32)
    spread_two[source, column] = 1
    mask_two = (column[None, :] % 8 == parent[:, None]).astype(np.float32)
    row = np.arange(128)
    c2x, c3x, c2y, c3y, c1z, c2z, c3z = [bit(row, 6 - i) for i in range(7)]
    pick_three = np.zeros((128, 64), np.float32)
    pick_three[row, 8 * (4 * c3x + 2 * c3y + c3z)] = 1
    column = np.arange(1024)
    source = np.where(column < 896, 8 + column // 16, (column - 896) // 16)
    spread_three = np.zeros((64, 1024), np.float32)
    spread_three[source, column] = 1
    own = 8 * c1z + 4 * c2x + 2 * c2y + c2z
    mask_three = (column[None, :] % 16 == own[:, None]).astype(np.float32)
    picks = [pick_one, pick_two, spread_two, mask_two, pick_three, spread_three, mask_three]
    return [np.asarray(each, jnp.bfloat16) for each in picks]


def slot_tables():
    slot = np.arange(128)
    y_part = 2 * (slot // 32) + slot % 2
    z_part = (slot // 2) % 16
    mode = np.arange(128)
    kz, ky = mode // 8, mode % 8
    angle = 2 * np.pi * (np.outer(kz, z_part) / 16 + np.outer(ky, y_part) / 8)
    high, low = two_terms(np.concatenate([np.cos(angle), np.sin(angle)], axis=1))
    both = np.concatenate([high, low], axis=0)
    turn = 2 * np.pi * np.outer(np.arange(4), y_part) / 32
    turns = np.stack([np.cos(turn), np.sin(turn)]).astype(np.float32)
    return both, turns


def line_tables():
    z_low = np.arange(128)
    out = []
    for kz_low in range(16):
        angle = 2 * np.pi * np.outer(z_low, kz_low + 16 * np.arange(128)) / 2048
        cos, sin = np.cos(angle), np.sin(angle)
        out.append(np.block([[cos, -sin], [sin, cos]]))
    return np.stack(two_terms(np.stack(out)), axis=1)


def turn_tables():
    kt = np.arange(4)[:, None]
    s = np.arange(8)[None, :]
    ky_low = kt + 4 * s
    one = 2 * np.pi * ky_low[:, None, :] * np.arange(8)[None, :, None] / 256
    mode = ky_low[:, None, None, :] + 32 * np.arange(8)[None, None, :, None]
    two = 2 * np.pi * mode * np.arange(8)[None, :, None, None] / 2048
    wide = lambda a: np.ascontiguousarray(
        np.broadcast_to(np.stack([np.cos(a), np.sin(a)])[..., None], (2,) + a.shape + (128,))
    ).astype(np.float32)
    return wide(one), wide(two)


def digit_tables():
    out = []
    for pair in range(2):
        full = np.zeros((2, 2, 8, 8, 2, 2, 8, 8))
        for k in range(2):
            y2a = np.arange(8)[:, None]
            s = np.arange(8)[None, :]
            angle = 2 * np.pi * (s * y2a / 8 + (2 * pair + k) * y2a / 32)
            cos, sin = np.cos(angle), np.sin(angle)
            for y0 in range(8):
                full[0, k, :, y0, 0, k, y0, :] = cos
                full[0, k, :, y0, 1, k, y0, :] = -sin
                full[1, k, :, y0, 0, k, y0, :] = sin
                full[1, k, :, y0, 1, k, y0, :] = cos
        high, low = two_terms(full.reshape(256, 256))
        out.append(np.concatenate([high, low], axis=0))
    return np.stack(out)


def split(x):
    high = x.astype(BF16)
    return high, (x - high.astype(F32)).astype(BF16)


def dot(a, b):
    return jnp.dot(a, b, preferred_element_type=F32)


def dot_nt(a, b):
    return lax.dot_general(a, b, (((1,), (1,)), ((), ())), preferred_element_type=F32)


def add(a, b):
    return (a[0] + b[0], a[1] + b[1])


def sub(a, b):
    return (a[0] - b[0], a[1] - b[1])


def times(a, cos, sin, sign):
    if sign > 0:
        return (a[0] * cos - a[1] * sin, a[1] * cos + a[0] * sin)
    return (a[0] * cos + a[1] * sin, a[1] * cos - a[0] * sin)


def quarter(a, sign):
    return (-a[1], a[0]) if sign > 0 else (a[1], -a[0])


def add_quarter(a, b, sign):
    return (a[0] - b[1], a[1] + b[0]) if sign > 0 else (a[0] + b[1], a[1] - b[0])


def four(x, sign):
    even, odd = add(x[0], x[2]), add(x[1], x[3])
    left, right = sub(x[0], x[2]), sub(x[1], x[3])
    return [add(even, odd), add_quarter(left, right, sign), sub(even, odd),
            add_quarter(left, right, -sign)]


def eight(x, sign):
    even = four([x[0], x[2], x[4], x[6]], sign)
    odd = four([x[1], x[3], x[5], x[7]], sign)
    half = math.sqrt(0.5)
    a = odd[1]
    if sign > 0:
        odd1 = ((a[0] - a[1]) * half, (a[1] + a[0]) * half)
    else:
        odd1 = ((a[0] + a[1]) * half, (a[1] - a[0]) * half)
    a = odd[3]
    if sign > 0:
        odd3 = ((-a[0] - a[1]) * half, (a[0] - a[1]) * half)
    else:
        odd3 = ((a[1] - a[0]) * half, (-a[0] - a[1]) * half)
    return [
        add(even[0], odd[0]),
        add(even[1], odd1),
        add_quarter(even[2], odd[2], sign),
        add(even[3], odd3),
        sub(even[0], odd[0]),
        sub(even[1], odd1),
        add_quarter(even[2], odd[2], -sign),
        sub(even[3], odd3),
    ]


def sixteen(x, sign):
    out = [None] * 16
    mid = [four([x[a], x[a + 4], x[a + 8], x[a + 12]], sign) for a in range(4)]
    for c in range(4):
        terms = []
        for a in range(4):
            angle = 2 * math.pi * a * c / 16
            if a * c == 0:
                terms.append(mid[a][c])
            elif a * c == 4:
                terms.append(quarter(mid[a][c], sign))
            else:
                terms.append(times(mid[a][c], math.cos(angle), math.sin(angle), sign))
        done = four(terms, sign)
        for d in range(4):
            out[c + 4 * d] = done[d]
    return out


def prepare(mixing, picks, first_map, second_map, leaf_map):
    pick_one, pick_two, spread_two, mask_two, pick_three, spread_three, mask_three = picks
    mix = mixing[...]
    first_map[...] = dot(pick_one[...], mix).astype(BF16)
    rows = dot(pick_two[...], mix).astype(BF16)
    second_map[...] = (dot(rows, spread_two[...]) * mask_two[...].astype(F32)).astype(BF16)
    rows = dot(pick_three[...], mix).astype(BF16)
    leaf_map[...] = (dot(rows, spread_three[...]) * mask_three[...].astype(F32)).astype(BF16)


def expand(half, lanes, top, one, two, draws, arrived_draws, first_map, second_map, leaf_map,
           slots, turns, parents, leaves, high_rows, low_rows, sent):
    records = jnp.concatenate([top[:, lanes], one[:, lanes].astype(F32)], axis=0)
    high, low = split(records)
    high, low = split(dot(first_map[...], high) + dot(first_map[...], low))
    level_two = dot(second_map[...], jnp.concatenate([two[:, lanes], high], axis=0))
    low = jnp.concatenate([jnp.zeros_like(low), low], axis=0)
    level_two = level_two + dot(second_map[:, 384:], low)
    for tile in range(4):
        high, low = split(level_two[tile * 128:(tile + 1) * 128])
        parents[tile, 0:128] = high
        parents[tile, 128:256] = low

    @pl.loop(0, 2)
    def _(c1x):
        for c1y in range(2):
            tile = 2 * c1x + c1y
            arrived_draws(half, tile).wait()
            rows = pl.ds(pl.multiple_of(tile * 16, 16), 16)
            got = dot(leaf_map[:, :896], draws[half, :, rows, :].reshape(896, 512))
            near = parents[tile]
            got = got + dot(leaf_map[:, 896:], near[:128]) + dot(leaf_map[:, 896:], near[128:])
            for group in range(4):
                leaves[group, c1y] = got[group * 32:(group + 1) * 32]
        for pair in range(2):
            quarters = []
            for t in range(4):
                lane = t * 128
                re = leaves[2 * pair, :, :, lane:lane + 128].reshape(64, 128)
                im = leaves[2 * pair + 1, :, :, lane:lane + 128].reshape(64, 128)
                quarters.append((re, im))
            for k, value in enumerate(four(quarters, -1)):
                if k:
                    value = times(value, turns[0, k:k + 1], turns[1, k:k + 1], -1)
                re_high, re_low = split(value[0])
                im_high, im_low = split(value[1])
                base = pair * 128
                high_rows[k, base:base + 64, 0:128] = re_high
                high_rows[k, base:base + 64, 128:256] = im_high
                high_rows[k, base + 64:base + 128, 0:128] = im_high
                high_rows[k, base + 64:base + 128, 128:256] = -re_high
                low_rows[k, base:base + 64, 0:128] = re_low
                low_rows[k, base:base + 64, 128:256] = im_low
                low_rows[k, base + 64:base + 128, 0:128] = im_low
                low_rows[k, base + 64:base + 128, 128:256] = -re_low
        for k in range(4):
            both = dot_nt(slots[...], high_rows[k])
            done = both[:128] + both[128:] + dot_nt(slots[0:128], low_rows[k])
            for pair in range(2):
                piece = done[:, pair * 128:(pair + 1) * 128].reshape(16, 8, 128)
                sent[half, 2 * c1x + pair, :, k] = piece


def owner_index(q, w):
    index = 0
    for b in range(4):
        index += bit(w, b) << (2 * b)
    for b in range(3):
        index += bit(q, b) << (2 * b + 1)
    return index


def swap_lanes(x, lane):
    for b in range(4):
        width = 8 << b
        keep = (lane & width) == 0
        y = list(x)
        for i in range(16):
            if not bit(i, b):
                j = i | (1 << b)
                y[i] = jnp.where(keep, x[i], pltpu.roll(x[j], width, 1))
                y[j] = jnp.where(keep, pltpu.roll(x[i], 128 - width, 1), x[j])
        x = y
    return x


def along_lines(kt, arrived, factor, table, turn_one, turn_two, lane, flat, mid, work, spread):
    @pl.loop(0, 8)
    def _(q):
        base = 2 * (q % 2) + 8 * ((q // 2) % 2) + 32 * (q // 4)
        places = [owner_index(0, w) for w in range(16)]
        got = swap_lanes([arrived[base + place, kt] for place in places], lane)
        for oy in range(8):
            rows = pl.ds(pl.multiple_of(q * 64 + oy * 8, 8), 8)
            flat[rows, 0:128] = got[oy]
            flat[rows, 128:256] = got[8 + oy]

    for part in range(2):
        rows = pl.ds(part * 256, 256)
        high, low = split(flat[rows, :])
        mid[rows, :] = dot(high, table[0]) + dot(low, table[0]) + dot(high, table[1])

    @pl.loop(0, 8)
    def _(oy):
        x = []
        for q in range(8):
            rows = pl.ds(pl.multiple_of(q * 64 + oy * 8, 8), 8)
            value = (mid[rows, 0:128], mid[rows, 128:256])
            if q:
                value = times(value, turn_one[0, kt, q], turn_one[1, kt, q], -1)
            x.append(value)
        for k, value in enumerate(eight(x, -1)):
            value = times(value, turn_two[0, kt, oy, k], turn_two[1, kt, oy, k], -1)
            work[0, k, oy] = value[0]
            work[1, k, oy] = value[1]

    @pl.loop(0, 8)
    def _(kq):
        x = eight([(work[0, kq, oy], work[1, kq, oy]) for oy in range(8)], -1)
        y = []
        for k in range(8):
            rows = pl.ds(pl.multiple_of((kt * 8 + k) * 64 + kq * 8, 8), 8)
            scale = factor[rows, :]
            y.append((x[k][0] * scale, x[k][1] * scale))
        for y0, value in enumerate(eight(y, 1)):
            value = times(value, turn_two[0, kt, y0, kq], turn_two[1, kt, y0, kq], 1)
            work[0, kq, y0] = value[0]
            work[1, kq, y0] = value[1]

    @pl.loop(0, 8)
    def _(y0):
        x = [(work[0, kq, y0], work[1, kq, y0]) for kq in range(8)]
        for y1, value in enumerate(eight(x, 1)):
            if y1:
                value = times(value, turn_one[0, kt, y1], turn_one[1, kt, y1], 1)
            spread[0, kt, y1, y0] = value[0]
            spread[1, kt, y1, y0] = value[1]


def next_digit(ktp, digits, spread, mixed):
    @pl.loop(0, 4)
    def _(pair):
        columns = []
        for one in range(2):
            pieces = [
                spread[part, 2 * ktp + k, 2 * pair + one].reshape(64, 128)
                for part in range(2)
                for k in range(2)
            ]
            columns.append(jnp.concatenate(pieces, axis=0))
        high, low = split(jnp.concatenate(columns, axis=1))
        both = dot(digits[ktp], high)
        mixed[ktp, pair] = both[:256] + both[256:] + dot(digits[ktp, 0:256], low)


def last_digit(mixed, lined):
    @pl.loop(0, 4)
    def _(pair):
        for y2a in range(8):
            for one in range(2):
                x = []
                for kt in range(4):
                    base = (kt % 2) * 64 + y2a * 8
                    lanes = slice(one * 128, one * 128 + 128)
                    x.append((mixed[kt // 2, pair, base:base + 8, lanes],
                              mixed[kt // 2, pair, 128 + base:128 + base + 8, lanes]))
                for y2b, value in enumerate(four(x, 1)):
                    rows = pl.ds(pl.multiple_of((y2b * 8 + y2a) * 64 + (2 * pair + one) * 8, 8), 8)
                    lined[rows, 0:128] = value[0]
                    lined[rows, 128:256] = value[1]


PHASES = ((0, 3), (3, 1))


def whole_kernel(top, one, two, mixing, *refs):
    picks, refs = refs[:7], refs[7:]
    (slots, turns, digits, three, transfer, lines, turn_one_far, turn_two_far, out,
     first_map, second_map, leaf_map, draws, parents, leaves, high_rows, low_rows, sent, arrived,
     modes, factor, table, turn_one, turn_two, flat, mid, work, spread, mixed, lined, ready,
     draw_sem, fetch_sem, send_sem, recv_sem, back_send, back_recv) = refs
    row, col = lax.axis_index("row"), lax.axis_index("col")
    me = row * 16 + col
    core, z, y_low = lax.rem(col, 2), lax.rem(col // 2, 4), col // 8
    x, y_high = lax.rem(row, 4), row // 4

    barrier = pltpu.get_barrier_semaphore()

    @pl.loop(1, 128)
    def _(k):
        other = lax.rem(me + k, 128)
        pl.semaphore_signal(barrier, inc=1, device_id=(other // 16, lax.rem(other, 16)),
                            device_id_type=MESH)

    def lanes_of(half):
        e = lax.rem(half + core, 2)
        return pl.ds(pl.multiple_of(e * 512, 512), 512)

    def draw_copy(half, tile):
        rows = pl.ds(pl.multiple_of(tile * 16, 16), 16)
        return pltpu.make_async_copy(three.at[:, rows, lanes_of(half)],
                                     draws.at[half, :, rows, :], draw_sem.at[half, tile])

    for half in range(2):
        for tile in range(4):
            draw_copy(half, tile).start()
    fetches = [
        pltpu.make_async_copy(transfer, modes, fetch_sem.at[0]),
        pltpu.make_async_copy(lines.at[col], table, fetch_sem.at[1]),
        pltpu.make_async_copy(turn_one_far, turn_one, fetch_sem.at[2]),
        pltpu.make_async_copy(turn_two_far, turn_two, fetch_sem.at[3]),
    ]
    for fetch in fetches:
        fetch.start()
    prepare(mixing, picks, first_map, second_map, leaf_map)

    def send(half, phase):
        first, count = PHASES[phase]
        kts = pl.ds(first, count)
        e = lax.rem(half + core, 2)

        @pl.loop(0, 64)
        def _(k):
            j = lax.rem(k * 37 + 37, 64)
            to_x = lax.rem(x + lax.rem(j, 4), 4)
            to_z = lax.rem(z + lax.rem(j // 4, 4), 4)
            to_y = lax.rem(y_low + lax.rem(j // 16, 2), 2)
            to_core = lax.rem(core + j // 32, 2)
            to_row, to_col = 4 * e + to_x, to_y * 8 + to_z * 2 + to_core
            here = jnp.logical_and(to_row == row, to_col == col)

            @pl.when(jnp.logical_not(here))
            def _():
                pltpu.make_async_remote_copy(
                    sent.at[half, to_x, to_col, kts], arrived.at[me, kts],
                    send_sem.at[half, phase], recv_sem.at[phase],
                    device_id=(to_row, to_col), device_id_type=MESH).start()

            @pl.when(here)
            def _():
                pltpu.make_async_copy(sent.at[half, to_x, to_col, kts], arrived.at[me, kts],
                                      send_sem.at[half, phase]).start()

    def sent_all(half, phase):
        first, count = PHASES[phase]
        view = sent.at[half, :, :, pl.ds(first, count)]
        pltpu.make_async_copy(view, view, send_sem.at[half, phase]).wait()

    def received_all(phase):
        first, count = PHASES[phase]
        view = arrived.at[pl.ds(0, 127), pl.ds(first, count)]
        pltpu.make_async_copy(view, view, recv_sem.at[phase]).wait()

    for half in range(2):
        expand(half, lanes_of(half), top, one, two, draws, draw_copy, first_map, second_map,
               leaf_map, slots, turns, parents, leaves, high_rows, low_rows, sent)
        if half == 0:
            pl.semaphore_wait(barrier, 127)
        send(half, 0)

    for fetch in fetches:
        fetch.wait()

    @pl.loop(0, 128)
    def _(i):
        low, kt, high = i // 32, lax.rem(i // 8, 4), lax.rem(i, 8)
        rows = modes[pl.ds(pl.multiple_of((low * 4 + kt) * 128 + high * 16, 16), 16), :]
        factor[pl.ds((kt * 8 + high) * 64 + low, 16, stride=4), :] = rows * (1.0 / (2048 * 2048))

    sent_all(0, 0)
    send(0, 1)
    sent_all(1, 0)
    send(1, 1)

    lane = lax.broadcasted_iota(jnp.int32, (8, 128), 1)
    for phase in range(2):
        if phase:
            sent_all(0, 1)
            sent_all(1, 1)
        received_all(phase)
        first, count = PHASES[phase]

        @pl.loop(first, first + count)
        def _(kt):
            along_lines(kt, arrived, factor, table, turn_one, turn_two, lane, flat, mid, work,
                        spread)

        next_digit(phase, digits, spread, mixed)

    last_digit(mixed, lined)

    @pl.loop(0, 16)
    def _(k):
        j = lax.rem(k * 7 + 7, 16)
        to_z = lax.rem(z + lax.rem(j // 2, 4), 4)
        to_y = lax.rem(y_low + lax.rem(j, 2), 2)
        to_core = lax.rem(core + j // 8, 2)
        to = to_y * 8 + to_z * 2 + to_core
        high, low = split(lined[pl.ds(pl.multiple_of(to * 128, 128), 128), :])
        both = dot_nt(jnp.concatenate([high, low], axis=0), table[0])
        done = both[:128] + both[128:] + dot_nt(high, table[1])
        ready[to, 0] = done[:, :128]
        ready[to, 1] = done[:, 128:]

        @pl.when(to != col)
        def _():
            pltpu.make_async_remote_copy(ready.at[to], out.at[col], back_send, back_recv,
                                         device_id=(row, to), device_id_type=MESH).start()

        @pl.when(to == col)
        def _():
            pltpu.make_async_copy(ready.at[to], out.at[col], back_send).start()

    pltpu.make_async_copy(ready, ready, back_send).wait()
    view = ready.at[pl.ds(0, 15)]
    pltpu.make_async_copy(view, view, back_recv).wait()


def whole(top, one, two, three, mixing, transfer):
    slots, turns = slot_tables()
    turn_one, turn_two = turn_tables()
    near = [top, one, two.reshape(448, 1024), mixing] + owner_tables()
    near += [slots, turns, digit_tables()]
    far = [three, transfer, line_tables(), turn_one, turn_two]
    inside, outside = pl.BlockSpec(memory_space=VMEM), pl.BlockSpec(memory_space=pl.ANY)
    dma = pltpu.SemaphoreType.DMA
    return pl.pallas_call(
        whole_kernel,
        in_specs=[inside] * len(near) + [outside] * len(far),
        out_specs=outside,
        out_shape=jax.ShapeDtypeStruct((16, 2, 128, 128), F32),
        scratch_shapes=[
            VMEM((64, 64), BF16),
            VMEM((512, 512), BF16),
            VMEM((128, 1024), BF16),
            VMEM((2, 56, 64, 512), BF16),
            VMEM((4, 256, 512), BF16),
            VMEM((4, 2, 32, 512), F32),
            VMEM((4, 256, 256), BF16),
            VMEM((4, 256, 256), BF16),
            VMEM((2, 4, 16, 4, 8, 128), F32),
            VMEM((128, 4, 8, 128), F32),
            VMEM((2048, 128), F32),
            VMEM((2048, 128), F32),
            VMEM((2, 256, 256), BF16),
            VMEM((2, 4, 8, 8, 128), F32),
            VMEM((2, 4, 8, 8, 8, 128), F32),
            VMEM((512, 256), F32),
            VMEM((512, 256), F32),
            VMEM((2, 8, 8, 8, 128), F32),
            VMEM((2, 4, 8, 8, 8, 128), F32),
            VMEM((2, 4, 256, 256), F32),
            VMEM((2048, 256), F32),
            VMEM((16, 2, 128, 128), F32),
            dma((2, 4)),
            dma((4,)),
            dma((2, 2)),
            dma((2,)),
            dma,
            dma,
        ],
        compiler_params=pltpu.CompilerParams(
            collective_id=0, has_side_effects=True, vmem_limit_bytes=56 * 2**20),
    )(*[jnp.asarray(a) for a in near + far])


def strip_kernel(arrived, out):
    @pl.loop(0, 4)
    def _(tile):
        rows = pl.ds(pl.multiple_of(tile * 8, 8), 8)
        x = [(arrived[k, 0, rows, :], arrived[k, 1, rows, :]) for k in range(16)]
        for z, value in enumerate(sixteen(x, 1)):
            out[0, rows, z * 128:(z + 1) * 128] = value[0]
            out[1, rows, z * 128:(z + 1) * 128] = value[1]


def strips(arrived):
    return pl.pallas_call(
        strip_kernel,
        grid=(4,),
        in_specs=[pl.BlockSpec((16, 2, 32, 128), lambda i: (0, 0, i, 0))],
        out_specs=pl.BlockSpec((2, 32, 2048), lambda i: (0, i, 0)),
        out_shape=jax.ShapeDtypeStruct((2, 128, 2048), F32),
        compiler_params=pltpu.CompilerParams(vmem_limit_bytes=32 * 2**20),
    )(arrived)


def body(top, one, two, three, mixing, transfer):
    return strips(whole(top, one, two, three, mixing, transfer))


def solution(mesh):
    return jax.shard_map(
        body,
        mesh=mesh,
        in_specs=(
            P(None, ("row", "col")),
            P(None, ("row", "col")),
            P(None, None, ("row", "col")),
            P(None, None, ("row", "col")),
            P(),
            P(None, "col"),
        ),
        out_specs=P("row", "col", None),
        check_vma=False,
    )
```

time: 103 us -> 85.3 us (0.83)
  the two profiles are of different devices: /device:TPU:1 before, /device:TPU:5 now
where the time goes in v1:
time: 85.3 us; the launch traced here: 85.1 us
  Pallas kernels  83.5 us (98%)
  local copies, waits for them, and re-layouts  1.58 us (2%)
    pallas_call x1, Pallas kernels, whole(): pl.pallas_call(whole_kernel, in_specs=[inside] * len(near) + [outside] *...  81.3 us
    pallas_call x1, Pallas kernels, strips(): pl.pallas_call(strip_kernel, grid=(4,), in_specs=[pl.BlockSpec((16, 2, 32...  2.21 us

profile of v1, /device:TPU:5, one launch (start us, length us, event | category | flops | bytes accessed | tf_op | source)
XLA Modules:
  0.0 85.1 jit_solution(17498325787737766639)
XLA Ops:
  0.0 81.3 %shard_map.181.arrived = f32[16,2,128,128]{3,2,1,0:T(8,128)} custom-call(f32[8,1024]{1,0:T(8,128)} %top.1, bf16[56,1024]{1,0:T(8,128)(2,1)} %one.1, bf16[448,1024]{1,0:T(8,128)(2,1)} %bitcast.1, bf16[64,64]{1,0:T(8,128)(2,1)} %mixing.1, bf16[64,64]{1,0:T(8,128)(2,1)} %constant.26.clone.refs_0_, bf16[512,64]{1,0:T(8,128)(2,1)} %constant.27.clone.refs_1_, ...), custom_call_target="tpu_custom_call" | custom-call | tf_op jit(solution)/shard_map/pallas_call | solution.py:524
  81.3 0.0 copy-start
  81.3 1.6 %copy-done = f32[16,2,128,128]{3,2,1,0:T(8,128)S(1)} copy-done((f32[16,2,128,128]{3,2,1,0:T(8,128)S(1)}, f32[16,2,128,128]{3,2,1,0:T(8,128)}, u32[]{:S(2)}) %copy-start) | copy-done | bytes 2097176
  82.9 2.2 %shard_map.182 = f32[2,128,2048]{2,1,0:T(8,128)} custom-call(f32[16,2,128,128]{3,2,1,0:T(8,128)S(1)} %copy-done), custom_call_target="tpu_custom_call" | custom-call | tf_op jit(solution)/shard_map/pallas_call | solution.py:575
Async XLA Ops:
  81.3 1.6 %copy-start = (f32[16,2,128,128]{3,2,1,0:T(8,128)S(1)}, f32[16,2,128,128]{3,2,1,0:T(8,128)}, u32[]{:S(2)}) copy-start(f32[16,2,128,128]{3,2,1,0:T(8,128)} %shard_map.181.arrived) | copy-start | bytes 6291460

commit v2 on v1

--- a/solution.py
+++ b/solution.py
@@ -30,26 +30,12 @@
     pick_one = np.zeros((64, 64), np.float32)
     pick_one[row, 8 * (row % 8) + row // 8] = 1
     row = np.arange(512)
-    cell, coef, parent = row % 8, (row >> 4) & 7, 2 * (row >> 7) + bit(row, 3)
     pick_two = np.zeros((512, 64), np.float32)
-    pick_two[row, 8 * cell + coef] = 1
-    column = np.arange(512)
-    source = np.where(column < 448, 8 + column // 8, (column - 448) // 8)
-    spread_two = np.zeros((64, 512), np.float32)
-    spread_two[source, column] = 1
-    mask_two = (column[None, :] % 8 == parent[:, None]).astype(np.float32)
+    pick_two[row, 8 * (row % 8) + ((row >> 4) & 7)] = 1
     row = np.arange(128)
-    c2x, c3x, c2y, c3y, c1z, c2z, c3z = [bit(row, 6 - i) for i in range(7)]
     pick_three = np.zeros((128, 64), np.float32)
-    pick_three[row, 8 * (4 * c3x + 2 * c3y + c3z)] = 1
-    column = np.arange(1024)
-    source = np.where(column < 896, 8 + column // 16, (column - 896) // 16)
-    spread_three = np.zeros((64, 1024), np.float32)
-    spread_three[source, column] = 1
-    own = 8 * c1z + 4 * c2x + 2 * c2y + c2z
-    mask_three = (column[None, :] % 16 == own[:, None]).astype(np.float32)
-    picks = [pick_one, pick_two, spread_two, mask_two, pick_three, spread_three, mask_three]
-    return [np.asarray(each, jnp.bfloat16) for each in picks]
+    pick_three[row, 8 * (4 * bit(row, 5) + 2 * bit(row, 3) + bit(row, 0))] = 1
+    return [np.asarray(each, jnp.bfloat16) for each in (pick_one, pick_two, pick_three)]
 
 
 def slot_tables():
@@ -58,22 +44,28 @@
     z_part = (slot // 2) % 16
     mode = np.arange(128)
     kz, ky = mode // 8, mode % 8
-    angle = 2 * np.pi * (np.outer(kz, z_part) / 16 + np.outer(ky, y_part) / 8)
-    high, low = two_terms(np.concatenate([np.cos(angle), np.sin(angle)], axis=1))
-    both = np.concatenate([high, low], axis=0)
+    angle = np.outer(kz, z_part) / 16 + np.outer(ky, y_part) / 8
+    angle = 2 * np.pi * (angle[None] + kz[None, :, None] * np.arange(16)[:, None, None] / 256)
+    high, low = two_terms(np.concatenate([np.cos(angle), np.sin(angle)], axis=2))
+    both = np.concatenate([high, low], axis=1)
     turn = 2 * np.pi * np.outer(np.arange(4), y_part) / 32
     turns = np.stack([np.cos(turn), np.sin(turn)]).astype(np.float32)
     return both, turns
 
 
 def line_tables():
-    z_low = np.arange(128)
-    out = []
+    z_low, kz_high = np.arange(128), np.arange(128)
+    sign = 1 - 2 * (kz_high % 2)
+    ahead, back = [], []
     for kz_low in range(16):
-        angle = 2 * np.pi * np.outer(z_low, kz_low + 16 * np.arange(128)) / 2048
+        angle = 2 * np.pi * np.outer(z_low, kz_low + 16 * kz_high) / 2048
         cos, sin = np.cos(angle), np.sin(angle)
-        out.append(np.block([[cos, -sin], [sin, cos]]))
-    return np.stack(two_terms(np.stack(out)), axis=1)
+        back.append(np.block([[cos, -sin], [sin, cos]]))
+        angle = np.outer(z_low, kz_high) / 128 + (z_low % 8)[:, None] * kz_low / 2048
+        cos, sin = np.cos(2 * np.pi * angle), np.sin(2 * np.pi * angle)
+        ahead.append(np.block([[cos, -sin], [sin * sign, cos * sign]]))
+    pair = lambda a: np.stack(two_terms(np.stack(a)), axis=1)
+    return pair(ahead), pair(back)
 
 
 def turn_tables():
@@ -86,7 +78,10 @@
     wide = lambda a: np.ascontiguousarray(
         np.broadcast_to(np.stack([np.cos(a), np.sin(a)])[..., None], (2,) + a.shape + (128,))
     ).astype(np.float32)
-    return wide(one), wide(two)
+    moved = two[..., None] - 2 * np.pi * np.multiply.outer(np.arange(8), np.arange(128))[
+        None, :, None, None, :] / 16
+    moved = np.stack([np.cos(moved), np.sin(moved)]).astype(np.float32)
+    return wide(one), wide(two), moved
 
 
 def digit_tables():
@@ -195,22 +190,31 @@
     return out
 
 
+def spread(rows, width, own):
+    shape = (64, 64 * width)
+    column = lax.broadcasted_iota(jnp.int32, shape, 1) // width
+    source = lax.broadcasted_iota(jnp.int32, shape, 0)
+    wide = dot(rows.astype(BF16), (((column + 8) & 63) == source).astype(F32).astype(BF16))
+    shape = (rows.shape[0], 64 * width)
+    cell = lax.broadcasted_iota(jnp.int32, shape, 1) & (width - 1)
+    return jnp.where(cell == own(lax.broadcasted_iota(jnp.int32, shape, 0)), wide, 0.0).astype(BF16)
+
+
 def prepare(mixing, picks, first_map, second_map, leaf_map):
-    pick_one, pick_two, spread_two, mask_two, pick_three, spread_three, mask_three = picks
     mix = mixing[...]
-    first_map[...] = dot(pick_one[...], mix).astype(BF16)
-    rows = dot(pick_two[...], mix).astype(BF16)
-    second_map[...] = (dot(rows, spread_two[...]) * mask_two[...].astype(F32)).astype(BF16)
-    rows = dot(pick_three[...], mix).astype(BF16)
-    leaf_map[...] = (dot(rows, spread_three[...]) * mask_three[...].astype(F32)).astype(BF16)
-
-
-def expand(half, lanes, top, one, two, draws, arrived_draws, first_map, second_map, leaf_map,
+    first_map[...] = dot(picks[0][...], mix).astype(BF16)
+    second_map[...] = spread(dot(picks[1][...], mix), 8, lambda r: 2 * (r >> 7) + bit(r, 3))
+    leaf_map[...] = spread(
+        dot(picks[2][...], mix), 16,
+        lambda r: 8 * bit(r, 2) + 4 * bit(r, 6) + 2 * bit(r, 4) + bit(r, 1))
+
+
+def expand(half, digit, lanes, top, one, two, draws, arrived_draws, first_map, second_map, leaf_map,
            slots, turns, parents, leaves, high_rows, low_rows, sent):
     records = jnp.concatenate([top[:, lanes], one[:, lanes].astype(F32)], axis=0)
     high, low = split(records)
     high, low = split(dot(first_map[...], high) + dot(first_map[...], low))
-    level_two = dot(second_map[...], jnp.concatenate([two[:, lanes], high], axis=0))
+    level_two = dot(second_map[...], jnp.concatenate([two[half], high], axis=0))
     low = jnp.concatenate([jnp.zeros_like(low), low], axis=0)
     level_two = level_two + dot(second_map[:, 384:], low)
     for tile in range(4):
@@ -228,28 +232,33 @@
             near = parents[tile]
             got = got + dot(leaf_map[:, 896:], near[:128]) + dot(leaf_map[:, 896:], near[128:])
             for group in range(4):
-                leaves[group, c1y] = got[group * 32:(group + 1) * 32]
-        for pair in range(2):
-            quarters = []
-            for t in range(4):
-                lane = t * 128
-                re = leaves[2 * pair, :, :, lane:lane + 128].reshape(64, 128)
-                im = leaves[2 * pair + 1, :, :, lane:lane + 128].reshape(64, 128)
-                quarters.append((re, im))
-            for k, value in enumerate(four(quarters, -1)):
-                if k:
-                    value = times(value, turns[0, k:k + 1], turns[1, k:k + 1], -1)
-                re_high, re_low = split(value[0])
-                im_high, im_low = split(value[1])
-                base = pair * 128
-                high_rows[k, base:base + 64, 0:128] = re_high
-                high_rows[k, base:base + 64, 128:256] = im_high
-                high_rows[k, base + 64:base + 128, 0:128] = im_high
-                high_rows[k, base + 64:base + 128, 128:256] = -re_high
-                low_rows[k, base:base + 64, 0:128] = re_low
-                low_rows[k, base:base + 64, 128:256] = im_low
-                low_rows[k, base + 64:base + 128, 0:128] = im_low
-                low_rows[k, base + 64:base + 128, 128:256] = -re_low
+                for i in range(4):
+                    row = group * 32 + i * 8
+                    leaves[group // 2, group % 2, 4 * c1y + i] = got[row:row + 8]
+
+        @pl.loop(0, 8)
+        def _(twin):
+            for pair in range(2):
+                quarters = []
+                for t in range(4):
+                    lane = slice(t * 128, t * 128 + 128)
+                    first, second = [], []
+                    for j in range(2):
+                        group = lax.rem(2 * twin + j - digit + 16, 16)
+                        part, oy = group // 8, lax.rem(group, 8)
+                        first.append(leaves[pair, part, oy, :, lane])
+                        other = leaves[pair, 1 - part, oy, :, lane]
+                        second.append(other * (1 - 2 * part).astype(F32))
+                    quarters.append((jnp.concatenate(first, axis=0), jnp.concatenate(second, axis=0)))
+                rows = pl.ds(pl.multiple_of(pair * 128 + twin * 16, 16), 16)
+                for k, value in enumerate(four(quarters, -1)):
+                    if k:
+                        value = times(value, turns[0, k:k + 1], turns[1, k:k + 1], -1)
+                    for side in range(2):
+                        high, low = split(value[side])
+                        high_rows[k, rows, side * 128:side * 128 + 128] = high
+                        low_rows[k, rows, side * 128:side * 128 + 128] = low
+
         for k in range(4):
             both = dot_nt(slots[...], high_rows[k])
             done = both[:128] + both[128:] + dot_nt(slots[0:128], low_rows[k])
@@ -267,26 +276,19 @@
     return index
 
 
-def swap_lanes(x, lane):
+def gather_lanes(x, lane):
     for b in range(4):
-        width = 8 << b
-        keep = (lane & width) == 0
-        y = list(x)
-        for i in range(16):
-            if not bit(i, b):
-                j = i | (1 << b)
-                y[i] = jnp.where(keep, x[i], pltpu.roll(x[j], width, 1))
-                y[j] = jnp.where(keep, pltpu.roll(x[i], 128 - width, 1), x[j])
-        x = y
-    return x
-
-
-def along_lines(kt, arrived, factor, table, turn_one, turn_two, lane, flat, mid, work, spread):
-    @pl.loop(0, 8)
+        here = (lane & (8 << b)) != 0
+        x = [jnp.where(here, x[(m + (1 << b)) % 16], x[m]) for m in range(16)]
+    return [x[(16 - d) % 16] for d in range(16)]
+
+
+def along_lines(kt, arrived, factor, table, turn_one, turn_two, moved, lane, flat, mid, work, placed):
+    @pl.loop(0, 8, unroll=2)
     def _(q):
         base = 2 * (q % 2) + 8 * ((q // 2) % 2) + 32 * (q // 4)
         places = [owner_index(0, w) for w in range(16)]
-        got = swap_lanes([arrived[base + place, kt] for place in places], lane)
+        got = gather_lanes([arrived[base + place, kt] for place in places], lane)
         for oy in range(8):
             rows = pl.ds(pl.multiple_of(q * 64 + oy * 8, 8), 8)
             flat[rows, 0:128] = got[oy]
@@ -297,7 +299,7 @@
         high, low = split(flat[rows, :])
         mid[rows, :] = dot(high, table[0]) + dot(low, table[0]) + dot(high, table[1])
 
-    @pl.loop(0, 8)
+    @pl.loop(0, 8, unroll=2)
     def _(oy):
         x = []
         for q in range(8):
@@ -307,11 +309,11 @@
                 value = times(value, turn_one[0, kt, q], turn_one[1, kt, q], -1)
             x.append(value)
         for k, value in enumerate(eight(x, -1)):
-            value = times(value, turn_two[0, kt, oy, k], turn_two[1, kt, oy, k], -1)
+            value = times(value, moved[0, kt, oy, k], moved[1, kt, oy, k], -1)
             work[0, k, oy] = value[0]
             work[1, k, oy] = value[1]
 
-    @pl.loop(0, 8)
+    @pl.loop(0, 8, unroll=2)
     def _(kq):
         x = eight([(work[0, kq, oy], work[1, kq, oy]) for oy in range(8)], -1)
         y = []
@@ -324,23 +326,23 @@
             work[0, kq, y0] = value[0]
             work[1, kq, y0] = value[1]
 
-    @pl.loop(0, 8)
+    @pl.loop(0, 8, unroll=2)
     def _(y0):
         x = [(work[0, kq, y0], work[1, kq, y0]) for kq in range(8)]
         for y1, value in enumerate(eight(x, 1)):
             if y1:
                 value = times(value, turn_one[0, kt, y1], turn_one[1, kt, y1], 1)
-            spread[0, kt, y1, y0] = value[0]
-            spread[1, kt, y1, y0] = value[1]
-
-
-def next_digit(ktp, digits, spread, mixed):
-    @pl.loop(0, 4)
+            placed[0, kt, y1, y0] = value[0]
+            placed[1, kt, y1, y0] = value[1]
+
+
+def next_digit(ktp, digits, placed, mixed):
+    @pl.loop(0, 4, unroll=True)
     def _(pair):
         columns = []
         for one in range(2):
             pieces = [
-                spread[part, 2 * ktp + k, 2 * pair + one].reshape(64, 128)
+                placed[part, 2 * ktp + k, 2 * pair + one].reshape(64, 128)
                 for part in range(2)
                 for k in range(2)
             ]
@@ -350,10 +352,10 @@
         mixed[ktp, pair] = both[:256] + both[256:] + dot(digits[ktp, 0:256], low)
 
 
-def last_digit(mixed, lined):
-    @pl.loop(0, 4)
+def last_digit(odd, mixed, lined):
+    @pl.loop(0, 4, unroll=True)
     def _(pair):
-        for y2a in range(8):
+        for y2a in range(odd, 8, 2):
             for one in range(2):
                 x = []
                 for kt in range(4):
@@ -370,16 +372,21 @@
 PHASES = ((0, 3), (3, 1))
 
 
-def whole_kernel(top, one, two, mixing, *refs):
-    picks, refs = refs[:7], refs[7:]
-    (slots, turns, digits, three, transfer, lines, turn_one_far, turn_two_far, out,
-     first_map, second_map, leaf_map, draws, parents, leaves, high_rows, low_rows, sent, arrived,
-     modes, factor, table, turn_one, turn_two, flat, mid, work, spread, mixed, lined, ready,
-     draw_sem, fetch_sem, send_sem, recv_sem, back_send, back_recv) = refs
+def whole_kernel(top, one, mixing, *refs):
+    picks, refs = refs[:3], refs[3:]
+    (turns, three, two_far, digits_far, slots_far, transfer, ahead_far, back_far, turn_one_far, turn_two_far,
+     moved_far, out,
+     first_map, second_map, leaf_map, two, digits, draws, parents, leaves, high_rows, low_rows, sent, arrived,
+     slots, modes, factor, ahead, back, turn_one, turn_two, moved, flat, mid, work, placed, mixed, lined, ready,
+     landed, strip,     draw_sem, fetch_sem, send_sem, recv_sem, back_send, back_recv,
+     out_sem, two_sem) = refs
     row, col = lax.axis_index("row"), lax.axis_index("col")
     me = row * 16 + col
     core, z, y_low = lax.rem(col, 2), lax.rem(col // 2, 4), col // 8
     x, y_high = lax.rem(row, 4), row // 4
+
+    digit = (lax.rem(col, 2) + 2 * lax.rem(col // 4, 2) + 4 * lax.rem(row, 2)
+             + 8 * lax.rem(row // 4, 2))
 
     barrier = pltpu.get_barrier_semaphore()
 
@@ -398,18 +405,26 @@
         return pltpu.make_async_copy(three.at[:, rows, lanes_of(half)],
                                      draws.at[half, :, rows, :], draw_sem.at[half, tile])
 
+    fetch_slots = pltpu.make_async_copy(slots_far.at[digit], slots, fetch_sem.at[6])
+    fetch_slots.start()
+    def two_copy(half):
+        return pltpu.make_async_copy(two_far.at[:, lanes_of(half)], two.at[half], two_sem.at[half])
+
     for half in range(2):
+        two_copy(half).start()
         for tile in range(4):
             draw_copy(half, tile).start()
     fetches = [
         pltpu.make_async_copy(transfer, modes, fetch_sem.at[0]),
-        pltpu.make_async_copy(lines.at[col], table, fetch_sem.at[1]),
+        pltpu.make_async_copy(ahead_far.at[col], ahead, fetch_sem.at[1]),
+        pltpu.make_async_copy(back_far.at[col], back, fetch_sem.at[4]),
+        pltpu.make_async_copy(moved_far, moved, fetch_sem.at[5]),
+        pltpu.make_async_copy(digits_far, digits, fetch_sem.at[7]),
         pltpu.make_async_copy(turn_one_far, turn_one, fetch_sem.at[2]),
         pltpu.make_async_copy(turn_two_far, turn_two, fetch_sem.at[3]),
     ]
-    for fetch in fetches:
-        fetch.start()
     prepare(mixing, picks, first_map, second_map, leaf_map)
+    fetch_slots.wait()
 
     def send(half, phase):
         first, count = PHASES[phase]
@@ -449,11 +464,15 @@
         pltpu.make_async_copy(view, view, recv_sem.at[phase]).wait()
 
     for half in range(2):
-        expand(half, lanes_of(half), top, one, two, draws, draw_copy, first_map, second_map,
+        two_copy(half).wait()
+        expand(half, digit, lanes_of(half), top, one, two, draws, draw_copy, first_map, second_map,
                leaf_map, slots, turns, parents, leaves, high_rows, low_rows, sent)
         if half == 0:
             pl.semaphore_wait(barrier, 127)
         send(half, 0)
+        if half == 0:
+            for fetch in fetches:
+                fetch.start()
 
     for fetch in fetches:
         fetch.wait()
@@ -479,68 +498,98 @@
 
         @pl.loop(first, first + count)
         def _(kt):
-            along_lines(kt, arrived, factor, table, turn_one, turn_two, lane, flat, mid, work,
-                        spread)
-
-        next_digit(phase, digits, spread, mixed)
-
-    last_digit(mixed, lined)
-
-    @pl.loop(0, 16)
-    def _(k):
-        j = lax.rem(k * 7 + 7, 16)
-        to_z = lax.rem(z + lax.rem(j // 2, 4), 4)
-        to_y = lax.rem(y_low + lax.rem(j, 2), 2)
-        to_core = lax.rem(core + j // 8, 2)
-        to = to_y * 8 + to_z * 2 + to_core
-        high, low = split(lined[pl.ds(pl.multiple_of(to * 128, 128), 128), :])
-        both = dot_nt(jnp.concatenate([high, low], axis=0), table[0])
-        done = both[:128] + both[128:] + dot_nt(high, table[1])
-        ready[to, 0] = done[:, :128]
-        ready[to, 1] = done[:, 128:]
-
-        @pl.when(to != col)
-        def _():
-            pltpu.make_async_remote_copy(ready.at[to], out.at[col], back_send, back_recv,
-                                         device_id=(row, to), device_id_type=MESH).start()
-
-        @pl.when(to == col)
-        def _():
-            pltpu.make_async_copy(ready.at[to], out.at[col], back_send).start()
-
-    pltpu.make_async_copy(ready, ready, back_send).wait()
-    view = ready.at[pl.ds(0, 15)]
-    pltpu.make_async_copy(view, view, back_recv).wait()
+            along_lines(kt, arrived, factor, ahead, turn_one, turn_two, moved, lane, flat, mid, work,
+                        placed)
+
+        next_digit(phase, digits, placed, mixed)
+
+    for odd in range(2):
+        last_digit(odd, mixed, lined)
+        half_strip = pl.ds(odd * 64, 64)
+
+        @pl.loop(0, 16)
+        def _(k):
+            j = lax.rem(k * 7 + 7, 16)
+            to_z = lax.rem(z + lax.rem(j // 2, 4), 4)
+            to_y = lax.rem(y_low + lax.rem(j, 2), 2)
+            to_core = lax.rem(core + j // 8, 2)
+            to = to_y * 8 + to_z * 2 + to_core
+            rows = pl.ds(pl.multiple_of(to * 128 + odd * 64, 64), 64)
+            high, low = split(lined[rows, :])
+            both = dot_nt(jnp.concatenate([high, low], axis=0), back[0])
+            done = both[:64] + both[64:] + dot_nt(high, back[1])
+            ready[to, 0, half_strip, :] = done[:, :128]
+            ready[to, 1, half_strip, :] = done[:, 128:]
+            source = ready.at[to, :, half_strip, :]
+            target = landed.at[col, :, half_strip, :]
+
+            @pl.when(to != col)
+            def _():
+                pltpu.make_async_remote_copy(
+                    source, target, back_send.at[odd], back_recv.at[odd],
+                    device_id=(row, to), device_id_type=MESH).start()
+
+            @pl.when(to == col)
+            def _():
+                pltpu.make_async_copy(source, target, back_send.at[odd]).start()
+
+    for odd in range(2):
+        half_strip = pl.ds(odd * 64, 64)
+        view = ready.at[:, :, half_strip, :]
+        pltpu.make_async_copy(view, view, back_send.at[odd]).wait()
+        view = ready.at[pl.ds(0, 15), :, half_strip, :]
+        pltpu.make_async_copy(view, view, back_recv.at[odd]).wait()
+
+        @pl.loop(0, 8)
+        def _(tile):
+            rows = pl.ds(pl.multiple_of(odd * 64 + tile * 8, 8), 8)
+            x = [(landed[k, 0, rows, :], landed[k, 1, rows, :]) for k in range(16)]
+            for place, value in enumerate(sixteen(x, 1)):
+                strip[0, rows, place * 128:(place + 1) * 128] = value[0]
+                strip[1, rows, place * 128:(place + 1) * 128] = value[1]
+
+        pltpu.make_async_copy(strip.at[:, half_strip, :], out.at[:, half_strip, :],
+                              out_sem.at[odd]).start()
+    for odd in range(2):
+        half_strip = pl.ds(odd * 64, 64)
+        pltpu.make_async_copy(strip.at[:, half_strip, :], out.at[:, half_strip, :],
+                              out_sem.at[odd]).wait()
 
 
 def whole(top, one, two, three, mixing, transfer):
     slots, turns = slot_tables()
-    turn_one, turn_two = turn_tables()
-    near = [top, one, two.reshape(448, 1024), mixing] + owner_tables()
-    near += [slots, turns, digit_tables()]
-    far = [three, transfer, line_tables(), turn_one, turn_two]
+    turn_one, turn_two, moved = turn_tables()
+    ahead, back = line_tables()
+    near = [top, one, mixing] + owner_tables()
+    near += [turns]
+    far = [three, two.reshape(448, 1024), digit_tables(), slots, transfer, ahead, back, turn_one, turn_two, moved]
     inside, outside = pl.BlockSpec(memory_space=VMEM), pl.BlockSpec(memory_space=pl.ANY)
     dma = pltpu.SemaphoreType.DMA
     return pl.pallas_call(
         whole_kernel,
         in_specs=[inside] * len(near) + [outside] * len(far),
         out_specs=outside,
-        out_shape=jax.ShapeDtypeStruct((16, 2, 128, 128), F32),
+        out_shape=jax.ShapeDtypeStruct((2, 128, 2048), F32),
         scratch_shapes=[
             VMEM((64, 64), BF16),
             VMEM((512, 512), BF16),
             VMEM((128, 1024), BF16),
+            VMEM((2, 448, 512), BF16),
+            VMEM((2, 512, 256), BF16),
             VMEM((2, 56, 64, 512), BF16),
             VMEM((4, 256, 512), BF16),
-            VMEM((4, 2, 32, 512), F32),
+            VMEM((2, 2, 8, 8, 512), F32),
             VMEM((4, 256, 256), BF16),
             VMEM((4, 256, 256), BF16),
             VMEM((2, 4, 16, 4, 8, 128), F32),
             VMEM((128, 4, 8, 128), F32),
+            VMEM((256, 256), BF16),
             VMEM((2048, 128), F32),
-            VMEM((2048, 128), F32),
+            VMEM((2056, 128), F32),
+            VMEM((2, 256, 256), BF16),
             VMEM((2, 256, 256), BF16),
             VMEM((2, 4, 8, 8, 128), F32),
+            VMEM((2, 4, 8, 8, 8, 128), F32),
             VMEM((2, 4, 8, 8, 8, 128), F32),
             VMEM((512, 256), F32),
             VMEM((512, 256), F32),
@@ -549,46 +598,25 @@
             VMEM((2, 4, 256, 256), F32),
             VMEM((2048, 256), F32),
             VMEM((16, 2, 128, 128), F32),
+            VMEM((16, 2, 128, 128), F32),
+            VMEM((2, 128, 2048), F32),
             dma((2, 4)),
-            dma((4,)),
+            dma((8,)),
             dma((2, 2)),
             dma((2,)),
-            dma,
-            dma,
+            dma((2,)),
+            dma((2,)),
+            dma((2,)),
+            dma((2,)),
         ],
         compiler_params=pltpu.CompilerParams(
             collective_id=0, has_side_effects=True, vmem_limit_bytes=56 * 2**20),
     )(*[jnp.asarray(a) for a in near + far])
 
 
-def strip_kernel(arrived, out):
-    @pl.loop(0, 4)
-    def _(tile):
-        rows = pl.ds(pl.multiple_of(tile * 8, 8), 8)
-        x = [(arrived[k, 0, rows, :], arrived[k, 1, rows, :]) for k in range(16)]
-        for z, value in enumerate(sixteen(x, 1)):
-            out[0, rows, z * 128:(z + 1) * 128] = value[0]
-            out[1, rows, z * 128:(z + 1) * 128] = value[1]
-
-
-def strips(arrived):
-    return pl.pallas_call(
-        strip_kernel,
-        grid=(4,),
-        in_specs=[pl.BlockSpec((16, 2, 32, 128), lambda i: (0, 0, i, 0))],
-        out_specs=pl.BlockSpec((2, 32, 2048), lambda i: (0, i, 0)),
-        out_shape=jax.ShapeDtypeStruct((2, 128, 2048), F32),
-        compiler_params=pltpu.CompilerParams(vmem_limit_bytes=32 * 2**20),
-    )(arrived)
-
-
-def body(top, one, two, three, mixing, transfer):
-    return strips(whole(top, one, two, three, mixing, transfer))
-
-
 def solution(mesh):
     return jax.shard_map(
-        body,
+        whole,
         mesh=mesh,
         in_specs=(
             P(None, ("row", "col")),

time: 85.3 us -> 73.2 us (0.86)
  the two profiles are of different devices: /device:TPU:5 before, /device:TPU:1 now
where the time goes in v2:
time: 73.2 us; the launch traced here: 73.1 us
  Pallas kernels  69.9 us (95%)
  local copies, waits for them, and re-layouts  3.14 us (4%)
    pallas_call x1, Pallas kernels, whole(): pl.pallas_call(whole_kernel, in_specs=[inside] * len(near) + [outside] *...  69.9 us
    unnamed x1, local copies, waits for them, and re-layouts  3.14 us

profile of v2, /device:TPU:1, one launch (start us, length us, event | category | flops | bytes accessed | tf_op | source)
XLA Modules:
  0.0 73.1 jit_solution(13847128186993259952)
XLA Ops:
  0.0 69.9 %shard_map.163 = f32[2,128,2048]{2,1,0:T(8,128)} custom-call(f32[8,1024]{1,0:T(8,128)} %top.1, bf16[56,1024]{1,0:T(8,128)(2,1)} %one.1, bf16[64,64]{1,0:T(8,128)(2,1)} %mixing.1, bf16[64,64]{1,0:T(8,128)(2,1)} %constant.22.clone.refs_0_, bf16[512,64]{1,0:T(8,128)(2,1)} %constant.23.clone.refs_1_, bf16[128,64]{1,0:T(8,128)(2,1)} %constant.24.clone.refs_2_, ...), custom_call_target="tpu_custom_call" | custom-call | tf_op jit(solution)/shard_map/pallas_call | solution.py:568
  69.9 3.1 %copy.19 = f32[2,128,2048]{2,1,0:T(8,128)} copy(f32[2,128,2048]{2,1,0:T(8,128)} %shard_map.163) | data formatting | bytes 4194304

commit v3 on v2

--- a/solution.py
+++ b/solution.py
@@ -378,8 +378,8 @@
      moved_far, out,
      first_map, second_map, leaf_map, two, digits, draws, parents, leaves, high_rows, low_rows, sent, arrived,
      slots, modes, factor, ahead, back, turn_one, turn_two, moved, flat, mid, work, placed, mixed, lined, ready,
-     landed, strip,     draw_sem, fetch_sem, send_sem, recv_sem, back_send, back_recv,
-     out_sem, two_sem) = refs
+          draw_sem, fetch_sem, send_sem, recv_sem, back_send, back_recv,
+     two_sem) = refs
     row, col = lax.axis_index("row"), lax.axis_index("col")
     me = row * 16 + col
     core, z, y_low = lax.rem(col, 2), lax.rem(col // 2, 4), col // 8
@@ -521,7 +521,7 @@
             ready[to, 0, half_strip, :] = done[:, :128]
             ready[to, 1, half_strip, :] = done[:, 128:]
             source = ready.at[to, :, half_strip, :]
-            target = landed.at[col, :, half_strip, :]
+            target = out.at[col, :, half_strip, :]
 
             @pl.when(to != col)
             def _():
@@ -540,20 +540,61 @@
         view = ready.at[pl.ds(0, 15), :, half_strip, :]
         pltpu.make_async_copy(view, view, back_recv.at[odd]).wait()
 
-        @pl.loop(0, 8)
+
+def strip_kernel(arrived, out, near, strip, sem, out_sem):
+    def fetch(part):
+        rows = pl.ds(part * 32, 32)
+        return [
+            pltpu.make_async_copy(arrived.at[pl.ds(8 * k, 8), :, rows, :],
+                                  near.at[pl.ds(8 * k, 8), :, rows, :], sem.at[part, k])
+            for k in range(2)
+        ]
+
+    def put(part):
+        rows = pl.ds(part * 32, 32)
+        return [
+            pltpu.make_async_copy(strip.at[plane, rows, :], out.at[plane, rows, :],
+                                  out_sem.at[part, plane])
+            for plane in range(2)
+        ]
+
+    for part in range(4):
+        for copy in fetch(part):
+            copy.start()
+    for part in range(4):
+        for copy in fetch(part):
+            copy.wait()
+
+        @pl.loop(0, 4, unroll=2)
         def _(tile):
-            rows = pl.ds(pl.multiple_of(odd * 64 + tile * 8, 8), 8)
-            x = [(landed[k, 0, rows, :], landed[k, 1, rows, :]) for k in range(16)]
+            rows = pl.ds(pl.multiple_of(part * 32 + tile * 8, 8), 8)
+            x = [(near[k, 0, rows, :], near[k, 1, rows, :]) for k in range(16)]
             for place, value in enumerate(sixteen(x, 1)):
                 strip[0, rows, place * 128:(place + 1) * 128] = value[0]
                 strip[1, rows, place * 128:(place + 1) * 128] = value[1]
 
-        pltpu.make_async_copy(strip.at[:, half_strip, :], out.at[:, half_strip, :],
-                              out_sem.at[odd]).start()
-    for odd in range(2):
-        half_strip = pl.ds(odd * 64, 64)
-        pltpu.make_async_copy(strip.at[:, half_strip, :], out.at[:, half_strip, :],
-                              out_sem.at[odd]).wait()
+        for copy in put(part):
+            copy.start()
+    for part in range(4):
+        for copy in put(part):
+            copy.wait()
+
+
+def body(*arrays):
+    outside = pl.BlockSpec(memory_space=pl.ANY)
+    return pl.pallas_call(
+        strip_kernel,
+        in_specs=[outside],
+        out_specs=outside,
+        out_shape=jax.ShapeDtypeStruct((2, 128, 2048), F32),
+        scratch_shapes=[
+            VMEM((16, 2, 128, 128), F32),
+            VMEM((2, 128, 2048), F32),
+            pltpu.SemaphoreType.DMA((4, 2)),
+            pltpu.SemaphoreType.DMA((4, 2)),
+        ],
+        compiler_params=pltpu.CompilerParams(vmem_limit_bytes=60 * 2**20),
+    )(whole(*arrays))
 
 
 def whole(top, one, two, three, mixing, transfer):
@@ -569,7 +610,7 @@
         whole_kernel,
         in_specs=[inside] * len(near) + [outside] * len(far),
         out_specs=outside,
-        out_shape=jax.ShapeDtypeStruct((2, 128, 2048), F32),
+        out_shape=jax.ShapeDtypeStruct((16, 2, 128, 128), F32),
         scratch_shapes=[
             VMEM((64, 64), BF16),
             VMEM((512, 512), BF16),
@@ -598,12 +639,9 @@
             VMEM((2, 4, 256, 256), F32),
             VMEM((2048, 256), F32),
             VMEM((16, 2, 128, 128), F32),
-            VMEM((16, 2, 128, 128), F32),
-            VMEM((2, 128, 2048), F32),
             dma((2, 4)),
             dma((8,)),
             dma((2, 2)),
-            dma((2,)),
             dma((2,)),
             dma((2,)),
             dma((2,)),
@@ -616,7 +654,7 @@
 
 def solution(mesh):
     return jax.shard_map(
-        whole,
+        body,
         mesh=mesh,
         in_specs=(
             P(None, ("row", "col")),

time: 73.2 us -> 71.5 us (0.977)
  local copies, waits for them, and re-layouts: 3.14 us -> 0 us
  Pallas kernels: 69.9 us -> 71.3 us
    unnamed x1 -> x0, local copies, waits for them, and re-layouts: 3.14 us -> none
    pallas_call x0 -> x1, Pallas kernels: none -> 2.6 us  [body(): pl.pallas_call(strip_kernel, in_specs=[outside], out_specs=outside, out_s...]
    pallas_call x1, Pallas kernels: 69.9 us -> 68.7 us  [whole(): pl.pallas_call(whole_kernel, in_specs=[inside] * len(near) + [outside] *...]
where the time goes in v3:
time: 71.5 us; the launch traced here: 71.3 us
  Pallas kernels  71.3 us (100%)
    pallas_call x1, Pallas kernels, whole(): pl.pallas_call(whole_kernel, in_specs=[inside] * len(near) + [outside] *...  68.7 us
    pallas_call x1, Pallas kernels, body(): pl.pallas_call(strip_kernel, in_specs=[outside], out_specs=outside, out_s...  2.6 us

profile of v3, /device:TPU:1, one launch (start us, length us, event | category | flops | bytes accessed | tf_op | source)
XLA Modules:
  0.0 71.3 jit_solution(15250454868482844118)
XLA Ops:
  0.0 68.7 %shard_map.163.arrived = f32[16,2,128,128]{3,2,1,0:T(8,128)} custom-call(f32[8,1024]{1,0:T(8,128)} %top.1, bf16[56,1024]{1,0:T(8,128)(2,1)} %one.1, bf16[64,64]{1,0:T(8,128)(2,1)} %mixing.1, bf16[64,64]{1,0:T(8,128)(2,1)} %constant.22.clone.refs_0_, bf16[512,64]{1,0:T(8,128)(2,1)} %constant.23.clone.refs_1_, bf16[128,64]{1,0:T(8,128)(2,1)} %constant.24.clone.refs_2_, ...), custom_call_target="tpu_custom_call" | custom-call | tf_op jit(solution)/shard_map/pallas_call | solution.py:609
  68.7 2.6 %shard_map.164 = f32[2,128,2048]{2,1,0:T(8,128)} custom-call(f32[16,2,128,128]{3,2,1,0:T(8,128)} %shard_map.163.arrived), custom_call_target="tpu_custom_call" | custom-call | tf_op jit(solution)/shard_map/pallas_call | solution.py:585

commit v4 on v3

--- a/solution.py
+++ b/solution.py
@@ -210,7 +210,7 @@
 
 
 def expand(half, digit, lanes, top, one, two, draws, arrived_draws, first_map, second_map, leaf_map,
-           slots, turns, parents, leaves, high_rows, low_rows, sent):
+           slots, turns, parents, leaves, high_rows, low_rows, sent, fetch_half):
     records = jnp.concatenate([top[:, lanes], one[:, lanes].astype(F32)], axis=0)
     high, low = split(records)
     high, low = split(dot(first_map[...], high) + dot(first_map[...], low))
@@ -221,6 +221,9 @@
         high, low = split(level_two[tile * 128:(tile + 1) * 128])
         parents[tile, 0:128] = high
         parents[tile, 128:256] = low
+
+    if half == 0:
+        fetch_half(1)
 
     @pl.loop(0, 2)
     def _(c1x):
@@ -236,7 +239,7 @@
                     row = group * 32 + i * 8
                     leaves[group // 2, group % 2, 4 * c1y + i] = got[row:row + 8]
 
-        @pl.loop(0, 8)
+        @pl.loop(0, 8, unroll=4)
         def _(twin):
             for pair in range(2):
                 quarters = []
@@ -410,10 +413,12 @@
     def two_copy(half):
         return pltpu.make_async_copy(two_far.at[:, lanes_of(half)], two.at[half], two_sem.at[half])
 
-    for half in range(2):
+    def fetch_half(half):
         two_copy(half).start()
         for tile in range(4):
             draw_copy(half, tile).start()
+
+    fetch_half(0)
     fetches = [
         pltpu.make_async_copy(transfer, modes, fetch_sem.at[0]),
         pltpu.make_async_copy(ahead_far.at[col], ahead, fetch_sem.at[1]),
@@ -433,7 +438,7 @@
 
         @pl.loop(0, 64)
         def _(k):
-            j = lax.rem(k * 37 + 37, 64)
+            j = lax.rem(k * 21 + 21, 64)
             to_x = lax.rem(x + lax.rem(j, 4), 4)
             to_z = lax.rem(z + lax.rem(j // 4, 4), 4)
             to_y = lax.rem(y_low + lax.rem(j // 16, 2), 2)
@@ -466,7 +471,7 @@
     for half in range(2):
         two_copy(half).wait()
         expand(half, digit, lanes_of(half), top, one, two, draws, draw_copy, first_map, second_map,
-               leaf_map, slots, turns, parents, leaves, high_rows, low_rows, sent)
+               leaf_map, slots, turns, parents, leaves, high_rows, low_rows, sent, fetch_half)
         if half == 0:
             pl.semaphore_wait(barrier, 127)
         send(half, 0)

time: 71.5 us -> 70.8 us (level)
  no operation moved by 1% of the time
where the time goes in v4:
time: 70.8 us; the launch traced here: 70.7 us
  Pallas kernels  70.7 us (100%)
    pallas_call x1, Pallas kernels, whole(): pl.pallas_call(whole_kernel, in_specs=[inside] * len(near) + [outside] *...  68.1 us
    pallas_call x1, Pallas kernels, body(): pl.pallas_call(strip_kernel, in_specs=[outside], out_specs=outside, out_s...  2.6 us

profile of v4, /device:TPU:1, one launch (start us, length us, event | category | flops | bytes accessed | tf_op | source)
XLA Modules:
  0.0 70.7 jit_solution(12787708785596774536)
XLA Ops:
  0.0 68.1 %shard_map.163.arrived = f32[16,2,128,128]{3,2,1,0:T(8,128)} custom-call(f32[8,1024]{1,0:T(8,128)} %top.1, bf16[56,1024]{1,0:T(8,128)(2,1)} %one.1, bf16[64,64]{1,0:T(8,128)(2,1)} %mixing.1, bf16[64,64]{1,0:T(8,128)(2,1)} %constant.22.clone.refs_0_, bf16[512,64]{1,0:T(8,128)(2,1)} %constant.23.clone.refs_1_, bf16[128,64]{1,0:T(8,128)(2,1)} %constant.24.clone.refs_2_, ...), custom_call_target="tpu_custom_call" | custom-call | tf_op jit(solution)/shard_map/pallas_call | solution.py:614
  68.1 2.6 %shard_map.164 = f32[2,128,2048]{2,1,0:T(8,128)} custom-call(f32[16,2,128,128]{3,2,1,0:T(8,128)} %shard_map.163.arrived), custom_call_target="tpu_custom_call" | custom-call | tf_op jit(solution)/shard_map/pallas_call | solution.py:590

commit v5 on v4

--- a/solution.py
+++ b/solution.py
@@ -548,7 +548,7 @@
 
 def strip_kernel(arrived, out, near, strip, sem, out_sem):
     def fetch(part):
-        rows = pl.ds(part * 32, 32)
+        rows = pl.ds(part * 16, 16)
         return [
             pltpu.make_async_copy(arrived.at[pl.ds(8 * k, 8), :, rows, :],
                                   near.at[pl.ds(8 * k, 8), :, rows, :], sem.at[part, k])
@@ -556,23 +556,23 @@
         ]
 
     def put(part):
-        rows = pl.ds(part * 32, 32)
+        rows = pl.ds(part * 16, 16)
         return [
             pltpu.make_async_copy(strip.at[plane, rows, :], out.at[plane, rows, :],
                                   out_sem.at[part, plane])
             for plane in range(2)
         ]
 
-    for part in range(4):
+    for part in range(8):
         for copy in fetch(part):
             copy.start()
-    for part in range(4):
+    for part in range(8):
         for copy in fetch(part):
             copy.wait()
 
-        @pl.loop(0, 4, unroll=2)
+        @pl.loop(0, 2, unroll=2)
         def _(tile):
-            rows = pl.ds(pl.multiple_of(part * 32 + tile * 8, 8), 8)
+            rows = pl.ds(pl.multiple_of(part * 16 + tile * 8, 8), 8)
             x = [(near[k, 0, rows, :], near[k, 1, rows, :]) for k in range(16)]
             for place, value in enumerate(sixteen(x, 1)):
                 strip[0, rows, place * 128:(place + 1) * 128] = value[0]
@@ -580,7 +580,7 @@
 
         for copy in put(part):
             copy.start()
-    for part in range(4):
+    for part in range(8):
         for copy in put(part):
             copy.wait()
 
@@ -595,8 +595,8 @@
         scratch_shapes=[
             VMEM((16, 2, 128, 128), F32),
             VMEM((2, 128, 2048), F32),
-            pltpu.SemaphoreType.DMA((4, 2)),
-            pltpu.SemaphoreType.DMA((4, 2)),
+            pltpu.SemaphoreType.DMA((8, 2)),
+            pltpu.SemaphoreType.DMA((8, 2)),
         ],
         compiler_params=pltpu.CompilerParams(vmem_limit_bytes=60 * 2**20),
     )(whole(*arrays))

time: 70.8 us -> 70.9 us (level)
  no operation moved by 1% of the time
where the time goes in v5:
time: 70.9 us; the launch traced here: 70.8 us
  Pallas kernels  70.7 us (100%)
    pallas_call x1, Pallas kernels, whole(): pl.pallas_call(whole_kernel, in_specs=[inside] * len(near) + [outside] *...  68.1 us
    pallas_call x1, Pallas kernels, body(): pl.pallas_call(strip_kernel, in_specs=[outside], out_specs=outside, out_s...  2.68 us

profile of v5, /device:TPU:1, one launch (start us, length us, event | category | flops | bytes accessed | tf_op | source)
XLA Modules:
  0.0 70.8 jit_solution(16991907161294236378)
XLA Ops:
  0.0 68.1 %shard_map.163.arrived = f32[16,2,128,128]{3,2,1,0:T(8,128)} custom-call(f32[8,1024]{1,0:T(8,128)} %top.1, bf16[56,1024]{1,0:T(8,128)(2,1)} %one.1, bf16[64,64]{1,0:T(8,128)(2,1)} %mixing.1, bf16[64,64]{1,0:T(8,128)(2,1)} %constant.22.clone.refs_0_, bf16[512,64]{1,0:T(8,128)(2,1)} %constant.23.clone.refs_1_, bf16[128,64]{1,0:T(8,128)(2,1)} %constant.24.clone.refs_2_, ...), custom_call_target="tpu_custom_call" | custom-call | tf_op jit(solution)/shard_map/pallas_call | solution.py:614
  68.1 2.7 %shard_map.164 = f32[2,128,2048]{2,1,0:T(8,128)} custom-call(f32[16,2,128,128]{3,2,1,0:T(8,128)} %shard_map.163.arrived), custom_call_target="tpu_custom_call" | custom-call | tf_op jit(solution)/shard_map/pallas_call | solution.py:590
